TPU v7x, 256 devices: a whole 4x4x8 slice. The times are simulated.
256 devices in a mesh: ctx: 64 (over z_lo, y, x), head: 4 (over z_hi, core).
Axes of the slice: x: 4, y: 4, z: 8 (z_hi: 2, z_lo: 4; z = z_hi * 4 + z_lo), core: 2. Of those that a mesh axis runs over, the one named last changes fastest.
Arguments:
- q_latent: bfloat16 [8192, 64, 512], P('ctx', 'head'), may hold values from -52 to 52
- q_rope: bfloat16 [8192, 4096], P('ctx', 'head'), may hold values from -6 to 6
- kv_latent: bfloat16 [8192, 512], P('ctx'), may hold values from -4 to 4
- k_rope: bfloat16 [8192, 64], P('ctx'), may hold values from -4 to 4
- out_grad: bfloat16 [8192, 64, 512], P('ctx', 'head'), may hold values from -6 to 6
- block_pos: int32 [128], replicated, may hold values from 0 to 127, each once
Outputs:
- grad_q_latent: bfloat16 [8192, 64, 512], P('ctx', 'head')
- grad_q_rope: bfloat16 [8192, 4096], P('ctx', 'head')
- grad_kv_latent: bfloat16 [8192, 512], P(('ctx', 'head'))
- grad_k_rope: bfloat16 [8192, 64], P(('ctx', 'head'))
Inputs may be any that keep to these rules, and one draw needn't show every extreme that they name: `block_pos`: each of the 128 context blocks appears once.
All inputs are finite; a program needn't handle non-finite values.
Results may differ from a plain program's by a relative error of at most 0.017.
Values may be sent and summed in bfloat16 or wider, within the bound.
A program may use at most 128 MiB of HBM per device.

v0:
```python
import functools

import jax
import jax.numpy as jnp
from jax import lax
from jax.experimental import pallas as pl
from jax.experimental.pallas import tpu as pltpu
from jax.sharding import PartitionSpec as P

SPAN = 4
LAT = 512
ROPE = 64
WIDE = 640
SCALE = 192.0 ** (-0.5)
SCALE_LOG2 = SCALE * 1.4426950408889634
CHUNK = 256
SPLITS = ((256, 384), (0, 256))

NT = (((1,), (1,)), ((), ()))
TN = (((0,), (0,)), ((), ()))


def dot(a, b, dims=(((1,), (0,)), ((), ()))):
    return lax.dot_general(a, b, dims, preferred_element_type=jnp.float32)


def kernel(
    n_ctx, heads,
    block_pos, kv_ref, kr_ref, qr_ref, q_hbm, g_hbm,
    dq_hbm, dqr_ref, dkv_ref, dkr_ref,
    kvr, qv, gv, rot32, s_a, s_b, dp_a, dp_b, ds_t, w_t, dq_st,
    d0, d1, as0, as1, ar0, ar1, bs0, bs1, br0, br1, cs0, cs1, cr0, cr1,
    in_sem, out_sem, f_send, f_recv, p_send, p_recv,
    a_send, a_recv, b_send, b_recv, c_send, c_recv,
):
    c = lax.axis_index("ctx")
    h = lax.axis_index("head")
    z = lax.div(h, 2)
    a = lax.rem(h, 2)
    sib = z * 2 + (1 - a)
    zpart = (1 - z) * 2 + a
    rows = qv.shape[0]
    n_chunks = rows // CHUNK
    half = rows // 2

    def ctx_at(k):
        return lax.rem(c + k + n_ctx, n_ctx)

    loads = [
        pltpu.make_async_copy(q_hbm, qv.at[:, pl.ds(0, LAT)], in_sem.at[0]),
        pltpu.make_async_copy(g_hbm, gv, in_sem.at[1]),
    ]
    for load in loads:
        load.start()

    barrier = pltpu.get_barrier_semaphore()
    peers = [(ctx_at(k), h) for k in (1, 2, 3, -1, -2, -3)] + [(c, sib), (c, zpart)]
    for peer in peers:
        pl.semaphore_signal(barrier, inc=1, device_id=peer, device_id_type=pl.DeviceIdType.MESH)

    kvr[0, :, :, pl.ds(0, LAT)] = kv_ref[...].reshape(2, 64, LAT)
    kvr[0, :, :, pl.ds(LAT, 128)] = jnp.concatenate(
        [kr_ref[...], jnp.zeros_like(kr_ref[...])], axis=1
    ).reshape(2, 64, 128)

    pl.semaphore_wait(barrier, len(peers))

    def remote(src, dst, send, recv, peer):
        return pltpu.make_async_remote_copy(
            src_ref=src, dst_ref=dst, send_sem=send, recv_sem=recv,
            device_id=peer, device_id_type=pl.DeviceIdType.MESH,
        )

    forward = {}
    for k in (2, 1, 3):
        forward[k] = remote(
            kvr.at[0, a], kvr.at[k, a], f_send.at[k - 1], f_recv.at[k - 1], (ctx_at(k), h)
        )
        forward[k].start()

    tokens = qr_ref.shape[0]
    low = lax.broadcasted_iota(jnp.int32, (tokens, 128), 1) < ROPE
    for j in range(heads // 2):
        tile = qr_ref[:, pl.ds(j * 128, 128)].astype(jnp.float32)
        rot32[pl.ds(2 * j, tokens, stride=heads), :] = jnp.where(low, tile, 0.0)
        rot32[pl.ds(2 * j + 1, tokens, stride=heads), :] = jnp.where(
            low, pltpu.roll(tile, 64, 1), 0.0
        )
    qv[:, pl.ds(LAT, 128)] = rot32[...].astype(jnp.bfloat16)

    passed = {}
    for k in (1, 3, 2):
        forward[k].wait_recv()
        passed[k] = remote(
            kvr.at[k, a], kvr.at[k, a], p_send.at[k - 1], p_recv.at[k - 1], (c, sib)
        )
        passed[k].start()
    for load in loads:
        load.wait()
    for k in (1, 3, 2):
        passed[k].wait_recv()

    key_pos = [
        block_pos[2 * ctx_at(-(slot // 2)) + slot % 2] for slot in range(2 * SPAN)
    ]
    query_pos = [block_pos[2 * c], block_pos[2 * c + 1]]

    def score(start, s_buf, dp_buf):
        at = pl.ds(start, CHUNK)
        keys = kvr[...].reshape(SPAN * 128, WIDE)
        s_buf[...] = dot(keys, qv[at, :], NT)
        dp_buf[...] = dot(keys[:, :LAT], gv[at, :], NT)

    lane_row = lax.broadcasted_iota(jnp.int32, (64, CHUNK), 1)
    sub_row = lax.broadcasted_iota(jnp.int32, (64, CHUNK), 0)

    def soften(start, s_buf, dp_buf):
        at = pl.ds(start, CHUNK)
        second = start // half
        pos = query_pos[second] * 64
        ahead = lax.div(lane_row + (start - second * half), heads) - sub_row
        top = None
        for slot in range(2 * SPAN):
            part = pl.ds(slot * 64, 64)
            seen = ahead >= key_pos[slot] * 64 - pos
            s = jnp.where(seen, s_buf[part, :], -jnp.inf)
            s_buf[part, :] = s
            m = jnp.max(s, axis=0, keepdims=True)
            top = m if top is None else jnp.maximum(top, m)
        total = None
        for slot in range(2 * SPAN):
            part = pl.ds(slot * 64, 64)
            e = jnp.exp2((s_buf[part, :] - top) * SCALE_LOG2)
            s_buf[part, :] = e
            t = jnp.sum(e, axis=0, keepdims=True)
            total = t if total is None else total + t
        inv = 1.0 / total
        delta = None
        for slot in range(2 * SPAN):
            part = pl.ds(slot * 64, 64)
            w = (s_buf[part, :] * inv).astype(jnp.bfloat16)
            w_t[part, at] = w
            t = jnp.sum(w.astype(jnp.float32) * dp_buf[part, :], axis=0, keepdims=True)
            delta = t if delta is None else delta + t
        for slot in range(2 * SPAN):
            part = pl.ds(slot * 64, 64)
            ds_t[part, at] = (
                (s_buf[part, :] * inv) * (dp_buf[part, :] - delta)
            ).astype(jnp.bfloat16)

    score(0, s_a, dp_a)

    def pair(i, _):
        start = i * (2 * CHUNK)
        score(start + CHUNK, s_b, dp_b)
        soften(start, s_a, dp_a)
        score((start + 2 * CHUNK) % rows, s_a, dp_a)
        soften(start + CHUNK, s_b, dp_b)
        return 0

    for i in range(n_chunks // 2):
        pair(i, 0)

    d, asb, arb, bsb, brb = (d0, d1), (as0, as1), (ar0, ar1), (bs0, bs1), (br0, br1)
    csb, crb = (cs0, cs1), (cr0, cr1)

    def key_grads(n):
        first, width = SPLITS[n]
        shape = (2 * SPAN, 2, 32, width)
        part = SCALE * dot(ds_t[...], qv[:, pl.ds(first, width)])
        latent = min(width, LAT - first)
        other = dot(w_t[...], gv[:, pl.ds(first, latent)])
        if latent == width:
            d[n][...] = (part + other).reshape(shape)
        else:
            d[n][:, :, :, pl.ds(0, latent)] = (part[:, :latent] + other).reshape(shape[:3] + (latent,))
            d[n][:, :, :, pl.ds(latent, width - latent)] = part[:, latent:].reshape(
                shape[:3] + (width - latent,)
            )
        asb[n][...] = d[n][:, pl.ds(1 - a, 1)].reshape(2 * SPAN, 32, width).astype(jnp.bfloat16)
        copy = remote(asb[n], arb[n], a_send.at[n], a_recv.at[n], (c, sib))
        copy.start()
        return copy

    def own(n, k):
        width = SPLITS[n][1]
        return d[n][pl.ds(2 * k, 2), pl.ds(a, 1)].reshape(2, 32, width)

    def add_cores(n, copy):
        copy.wait_recv()
        sends = []
        for k in (2, 1, 3):
            got = arb[n][pl.ds(2 * k, 2)].astype(jnp.float32)
            bsb[n][k - 1] = (own(n, k) + got).astype(jnp.bfloat16)
            sends.append(remote(
                bsb[n].at[k - 1], brb[n].at[k - 1], b_send.at[n, k - 1], b_recv.at[n, k - 1],
                (ctx_at(-k), h),
            ))
            sends[-1].start()
        return sends

    def add_context(n, sends):
        for copy in sends:
            copy.wait_recv()
        sums = own(n, 0) + arb[n][pl.ds(0, 2)].astype(jnp.float32)
        for k in (1, 2, 3):
            sums = sums + brb[n][k - 1].astype(jnp.float32)
        width = SPLITS[n][1]
        d[n][pl.ds(0, 2), pl.ds(a, 1)] = sums.reshape(2, 1, 32, width)
        csb[n][...] = d[n][pl.ds(1 - z, 1), pl.ds(a, 1)].reshape(32, width).astype(jnp.bfloat16)
        copy = remote(csb[n], crb[n], c_send.at[n], c_recv.at[n], (c, zpart))
        copy.start()
        return copy

    def finish(n, copy):
        copy.wait_recv()
        first, width = SPLITS[n]
        result = d[n][pl.ds(z, 1), pl.ds(a, 1)].reshape(32, width) + crb[n][...].astype(jnp.float32)
        result = result.astype(jnp.bfloat16)
        latent = min(width, LAT - first)
        dkv_ref[:, pl.ds(first, latent)] = result[:, :latent]
        if latent < width:
            dkr_ref[...] = result[:, latent:latent + ROPE]

    def query_grads(i):
        start = i * CHUNK
        at = pl.ds(start, CHUNK)
        keys = kvr[...].reshape(SPAN * 128, WIDE)
        grad = SCALE * dot(ds_t[:, at], keys, TN)
        dq_st[at, :] = grad[:, :LAT].astype(jnp.bfloat16)
        rot32[at, :] = grad[:, LAT:]

    def store(i):
        at = pl.ds(i * CHUNK, CHUNK)
        return pltpu.make_async_copy(dq_st.at[at, :], dq_hbm.at[at, :], out_sem.at[i])

    stores = []

    def query_step(i):
        query_grads(i)
        stores.append(store(i))
        stores[-1].start()

    a0 = key_grads(0)
    a1 = key_grads(1)
    b0 = add_cores(0, a0)
    query_step(0)
    query_step(1)
    b1 = add_cores(1, a1)
    query_step(2)
    query_step(3)
    query_step(4)
    c0 = add_context(0, b0)
    query_step(5)
    query_step(6)
    query_step(7)

    for j in range(heads // 2):
        even = rot32[pl.ds(2 * j, tokens, stride=heads), :]
        odd = rot32[pl.ds(2 * j + 1, tokens, stride=heads), :]
        dqr_ref[:, pl.ds(j * 128, 128)] = jnp.where(
            low, even, pltpu.roll(odd, 64, 1)
        ).astype(jnp.bfloat16)

    c1 = add_context(1, b1)
    finish(0, c0)
    for copy in [*forward.values(), *passed.values(), a0, a1, *b0, *b1, c0]:
        copy.wait_send()
    for copy in stores:
        copy.wait()
    finish(1, c1)
    c1.wait_send()


def per_device(q_latent, q_rope, kv_latent, k_rope, out_grad, block_pos):
    tokens, heads, lat = q_latent.shape
    rows = tokens * heads
    keys = SPAN * tokens
    n_ctx = lax.axis_size("ctx")
    bf16, f32 = jnp.bfloat16, jnp.float32
    vmem = pl.BlockSpec(memory_space=pltpu.VMEM)
    hbm = pl.BlockSpec(memory_space=pl.ANY)
    smem = pl.BlockSpec(memory_space=pltpu.SMEM)
    widths = [width for _, width in SPLITS]

    def pairs(shape, kind):
        return [pltpu.VMEM(shape + (width,), kind) for width in widths]

    dma = pltpu.SemaphoreType.DMA
    scratch = [
        pltpu.VMEM((SPAN, 2, 64, WIDE), bf16),
        pltpu.VMEM((rows, WIDE), bf16),
        pltpu.VMEM((rows, lat), bf16),
        pltpu.VMEM((rows, 128), f32),
        *[pltpu.VMEM((keys, CHUNK), f32) for _ in range(4)],
        pltpu.VMEM((keys, rows), bf16),
        pltpu.VMEM((keys, rows), bf16),
        pltpu.VMEM((rows, lat), bf16),
        *pairs((2 * SPAN, 2, 32), f32),
        *pairs((2 * SPAN, 32), bf16),
        *pairs((2 * SPAN, 32), bf16),
        *pairs((3, 2, 32), bf16),
        *pairs((3, 2, 32), bf16),
        *pairs((32,), bf16),
        *pairs((32,), bf16),
        dma((2,)), dma((rows // CHUNK,)),
        dma((3,)), dma((3,)), dma((3,)), dma((3,)),
        dma((2,)), dma((2,)), dma((2, 3)), dma((2, 3)), dma((2,)), dma((2,)),
    ]
    macs = rows * keys * (WIDE * 3 + 2 * lat)
    dq, dqr, dkv, dkr = pl.pallas_call(
        functools.partial(kernel, n_ctx, heads),
        out_shape=(
            jax.ShapeDtypeStruct((rows, lat), bf16),
            jax.ShapeDtypeStruct((tokens, heads * ROPE), bf16),
            jax.ShapeDtypeStruct((tokens // 4, lat), bf16),
            jax.ShapeDtypeStruct((tokens // 4, ROPE), bf16),
        ),
        in_specs=[smem, vmem, vmem, vmem, hbm, hbm],
        out_specs=(hbm, vmem, vmem, vmem),
        scratch_shapes=scratch,
        compiler_params=pltpu.CompilerParams(
            collective_id=0, has_side_effects=True, vmem_limit_bytes=48 * 2**20
        ),
        cost_estimate=pl.CostEstimate(
            flops=2 * macs, bytes_accessed=7 * 2**20, transcendentals=rows * keys
        ),
    )(
        block_pos, kv_latent, k_rope, q_rope,
        q_latent.reshape(rows, lat), out_grad.reshape(rows, lat),
    )
    return dq.reshape(tokens, heads, lat), dqr, dkv, dkr


def solution(mesh):
    in_specs = (
        P("ctx", "head", None),
        P("ctx", "head"),
        P("ctx", None),
        P("ctx", None),
        P("ctx", "head", None),
        P(),
    )
    out_specs = (
        P("ctx", "head", None),
        P("ctx", "head"),
        P(("ctx", "head"), None),
        P(("ctx", "head"), None),
    )
    return jax.shard_map(
        per_device, mesh=mesh, in_specs=in_specs, out_specs=out_specs, check_vma=False
    )
```

profile of v0, /device:TPU:1, one launch (start us, length us, event | category | flops | bytes accessed | tf_op | source)
XLA Modules:
  0.0 48.9 jit_solution(18280748572403931213)
XLA Ops:
  0.6 0.8 %copy.10.kr_ref = bf16[128,64]{1,0:T(8,128)(2,1)S(1)} copy(bf16[128,64]{0,1:T(8,128)(2,1)} %param.9) | data formatting | bytes 32768 | tf_op args[3]
  1.5 0.0 copy-start
  1.5 1.6 %copy-done = bf16[128,16,512]{2,1,0:T(8,128)(2,1)S(1)} copy-done((bf16[128,16,512]{2,1,0:T(8,128)(2,1)S(1)}, bf16[128,16,512]{2,1,0:T(8,128)(2,1)}, u32[]{:S(2)}) %copy-start) | copy-done | bytes 2097176
  3.1 0.0 copy-start.1
  3.1 0.9 %copy-done.1 = bf16[128,1024]{1,0:T(8,128)(2,1)S(1)} copy-done((bf16[128,1024]{1,0:T(8,128)(2,1)S(1)}, bf16[128,1024]{1,0:T(8,128)(2,1)}, u32[]{:S(2)}) %copy-start.1) | copy-done | bytes 262168
  4.0 0.0 copy-start.2
  4.0 0.9 %copy-done.2 = bf16[128,512]{1,0:T(8,128)(2,1)S(1)} copy-done((bf16[128,512]{1,0:T(8,128)(2,1)S(1)}, bf16[128,512]{1,0:T(8,128)(2,1)}, u32[]{:S(2)}) %copy-start.2) | copy-done | bytes 131096
  4.9 0.0 copy-start.3
  4.9 0.7 %copy-done.3 = s32[128]{0:T(128)S(1)} copy-done((s32[128]{0:T(128)S(1)}, s32[128]{0:T(128)}, u32[]{:S(2)}) %copy-start.3) | copy-done | bytes 536
  5.6 40.0 %shard_map.93 = (bf16[2048,512]{1,0:T(8,128)(2,1)S(1)}, bf16[128,1024]{1,0:T(8,128)(2,1)S(1)}, bf16[32,512]{1,0:T(8,128)(2,1)S(1)}, bf16[32,64]{1,0:T(8,128)(2,1)S(1)}) custom-call(s32[128]{0:T(128)S(1)} %copy-done.3, bf16[128,512]{1,0:T(8,128)(2,1)S(1)} %copy-done.2, bf16[128,64]{1,0:T(8,128)(2,1)S(1)} %copy.10.kr_ref, bf16[128,1024]{1,0:T(8,128)(2,1)S(1)} %copy-done.1, ...), custom_call_target="tpu_custom_call" | custom-call | flops 6174015488 | bytes 7340032 | tf_op jit(solution)/shard_map/pallas_call | solution.py:311
  45.6 1.3 %copy.15 = bf16[128,16,512]{2,1,0:T(8,128)(2,1)} copy(bf16[128,16,512]{2,1,0:T(8,128)(2,1)S(1)} %bitcast.3) | data formatting | bytes 4194304
  46.9 0.7 %copy.16 = bf16[128,1024]{1,0:T(8,128)(2,1)} copy(bf16[128,1024]{1,0:T(8,128)(2,1)S(1)} %get-tuple-element.17) | data formatting | bytes 524288
  47.6 0.6 %copy.17 = bf16[32,512]{1,0:T(8,128)(2,1)} copy(bf16[32,512]{1,0:T(8,128)(2,1)S(1)} %get-tuple-element.18) | data formatting | bytes 65536
  48.3 0.6 %copy.18 = bf16[32,64]{1,0:T(8,128)(2,1)} copy(bf16[32,64]{1,0:T(8,128)(2,1)S(1)} %get-tuple-element.19) | data formatting | bytes 8192
Async XLA Ops:
  1.5 1.6 %copy-start = (bf16[128,16,512]{2,1,0:T(8,128)(2,1)S(1)}, bf16[128,16,512]{2,1,0:T(8,128)(2,1)}, u32[]{:S(2)}) copy-start(bf16[128,16,512]{2,1,0:T(8,128)(2,1)} %param.6) | copy-start | bytes 6291460
  3.1 0.9 %copy-start.1 = (bf16[128,1024]{1,0:T(8,128)(2,1)S(1)}, bf16[128,1024]{1,0:T(8,128)(2,1)}, u32[]{:S(2)}) copy-start(bf16[128,1024]{1,0:T(8,128)(2,1)} %qr_ref.1) | copy-start | bytes 786436
  4.0 0.9 %copy-start.2 = (bf16[128,512]{1,0:T(8,128)(2,1)S(1)}, bf16[128,512]{1,0:T(8,128)(2,1)}, u32[]{:S(2)}) copy-start(bf16[128,512]{1,0:T(8,128)(2,1)} %kv_ref.1) | copy-start | bytes 393220
  4.9 0.7 %copy-start.3 = (s32[128]{0:T(128)S(1)}, s32[128]{0:T(128)}, u32[]{:S(2)}) copy-start(s32[128]{0:T(128)} %block_pos.1) | copy-start | bytes 1540
where the time goes:
time: 49.1 us; the launch traced here: 48.9 us
  Pallas kernels  40 us (81%)
  local copies, waits for them, and re-layouts  8.16 us (17%)
  between operations  0.65 us (1%)
    pallas_call x1, Pallas kernels, per_device(): pl.pallas_call(functools.partial(kernel, n_ctx, heads), out_shape=(jax.Sh...  40 us
    unnamed x13, local copies, waits for them, and re-layouts  8.16 us

commit v1 on v0

--- a/solution.py
+++ b/solution.py
@@ -26,11 +26,11 @@
 
 def kernel(
     n_ctx, heads,
-    block_pos, kv_ref, kr_ref, qr_ref, q_hbm, g_hbm,
-    dq_hbm, dqr_ref, dkv_ref, dkr_ref,
-    kvr, qv, gv, rot32, s_a, s_b, dp_a, dp_b, ds_t, w_t, dq_st,
+    pos_hbm, kv_hbm, kr_hbm, qr_hbm, q_hbm, g_hbm,
+    dq_ref, dqr_ref, dkv_ref, dkr_ref,
+    block_pos, kv_ref, kr_ref, qr_ref, kvr, qv, gv, rot32, s_a, s_b, dp_a, dp_b, ds_t, w_t,
     d0, d1, as0, as1, ar0, ar1, bs0, bs1, br0, br1, cs0, cs1, cr0, cr1,
-    in_sem, out_sem, f_send, f_recv, p_send, p_recv,
+    in_sem, f_send, f_recv, p_send, p_recv,
     a_send, a_recv, b_send, b_recv, c_send, c_recv,
 ):
     c = lax.axis_index("ctx")
@@ -40,17 +40,22 @@
     sib = z * 2 + (1 - a)
     zpart = (1 - z) * 2 + a
     rows = qv.shape[0]
-    n_chunks = rows // CHUNK
     half = rows // 2
 
     def ctx_at(k):
         return lax.rem(c + k + n_ctx, n_ctx)
 
+    load_keys = [
+        pltpu.make_async_copy(kv_hbm, kv_ref, in_sem.at[0]),
+        pltpu.make_async_copy(kr_hbm, kr_ref, in_sem.at[1]),
+    ]
+    load_rot = pltpu.make_async_copy(qr_hbm, qr_ref, in_sem.at[2])
     loads = [
-        pltpu.make_async_copy(q_hbm, qv.at[:, pl.ds(0, LAT)], in_sem.at[0]),
-        pltpu.make_async_copy(g_hbm, gv, in_sem.at[1]),
-    ]
-    for load in loads:
+        pltpu.make_async_copy(pos_hbm, block_pos, in_sem.at[3]),
+        pltpu.make_async_copy(q_hbm, qv.at[:, pl.ds(0, LAT)], in_sem.at[4]),
+        pltpu.make_async_copy(g_hbm, gv, in_sem.at[5]),
+    ]
+    for load in [*load_keys, load_rot, *loads]:
         load.start()
 
     barrier = pltpu.get_barrier_semaphore()
@@ -58,10 +63,13 @@
     for peer in peers:
         pl.semaphore_signal(barrier, inc=1, device_id=peer, device_id_type=pl.DeviceIdType.MESH)
 
+    for load in load_keys:
+        load.wait()
     kvr[0, :, :, pl.ds(0, LAT)] = kv_ref[...].reshape(2, 64, LAT)
+    rot = kr_ref[...].astype(jnp.float32)
     kvr[0, :, :, pl.ds(LAT, 128)] = jnp.concatenate(
-        [kr_ref[...], jnp.zeros_like(kr_ref[...])], axis=1
-    ).reshape(2, 64, 128)
+        [rot, jnp.zeros_like(rot)], axis=0
+    ).T.astype(jnp.bfloat16).reshape(2, 64, 128)
 
     pl.semaphore_wait(barrier, len(peers))
 
@@ -78,6 +86,7 @@
         )
         forward[k].start()
 
+    load_rot.wait()
     tokens = qr_ref.shape[0]
     low = lax.broadcasted_iota(jnp.int32, (tokens, 128), 1) < ROPE
     for j in range(heads // 2):
@@ -150,16 +159,12 @@
 
     score(0, s_a, dp_a)
 
-    def pair(i, _):
-        start = i * (2 * CHUNK)
+    for start in range(0, rows, 2 * CHUNK):
         score(start + CHUNK, s_b, dp_b)
         soften(start, s_a, dp_a)
-        score((start + 2 * CHUNK) % rows, s_a, dp_a)
+        if start + 2 * CHUNK < rows:
+            score(start + 2 * CHUNK, s_a, dp_a)
         soften(start + CHUNK, s_b, dp_b)
-        return 0
-
-    for i in range(n_chunks // 2):
-        pair(i, 0)
 
     d, asb, arb, bsb, brb = (d0, d1), (as0, as1), (ar0, ar1), (bs0, bs1), (br0, br1)
     csb, crb = (cs0, cs1), (cr0, cr1)
@@ -227,33 +232,22 @@
         at = pl.ds(start, CHUNK)
         keys = kvr[...].reshape(SPAN * 128, WIDE)
         grad = SCALE * dot(ds_t[:, at], keys, TN)
-        dq_st[at, :] = grad[:, :LAT].astype(jnp.bfloat16)
+        dq_ref[at, :] = grad[:, :LAT].astype(jnp.bfloat16)
         rot32[at, :] = grad[:, LAT:]
-
-    def store(i):
-        at = pl.ds(i * CHUNK, CHUNK)
-        return pltpu.make_async_copy(dq_st.at[at, :], dq_hbm.at[at, :], out_sem.at[i])
-
-    stores = []
-
-    def query_step(i):
-        query_grads(i)
-        stores.append(store(i))
-        stores[-1].start()
 
     a0 = key_grads(0)
     a1 = key_grads(1)
     b0 = add_cores(0, a0)
-    query_step(0)
-    query_step(1)
+    query_grads(0)
+    query_grads(1)
     b1 = add_cores(1, a1)
-    query_step(2)
-    query_step(3)
-    query_step(4)
+    query_grads(2)
+    query_grads(3)
+    query_grads(4)
     c0 = add_context(0, b0)
-    query_step(5)
-    query_step(6)
-    query_step(7)
+    query_grads(5)
+    query_grads(6)
+    query_grads(7)
 
     for j in range(heads // 2):
         even = rot32[pl.ds(2 * j, tokens, stride=heads), :]
@@ -266,10 +260,19 @@
     finish(0, c0)
     for copy in [*forward.values(), *passed.values(), a0, a1, *b0, *b1, c0]:
         copy.wait_send()
-    for copy in stores:
-        copy.wait()
     finish(1, c1)
     c1.wait_send()
+
+
+def move(*refs):
+    sources, targets, sem = refs[:4], refs[4:8], refs[8]
+    copies = [
+        pltpu.make_async_copy(s, t, sem.at[i]) for i, (s, t) in enumerate(zip(sources, targets))
+    ]
+    for copy in copies:
+        copy.start()
+    for copy in copies:
+        copy.wait()
 
 
 def per_device(q_latent, q_rope, kv_latent, k_rope, out_grad, block_pos):
@@ -279,8 +282,7 @@
     n_ctx = lax.axis_size("ctx")
     bf16, f32 = jnp.bfloat16, jnp.float32
     vmem = pl.BlockSpec(memory_space=pltpu.VMEM)
-    hbm = pl.BlockSpec(memory_space=pl.ANY)
-    smem = pl.BlockSpec(memory_space=pltpu.SMEM)
+    hbm = pl.BlockSpec(memory_space=pltpu.HBM)
     widths = [width for _, width in SPLITS]
 
     def pairs(shape, kind):
@@ -288,6 +290,10 @@
 
     dma = pltpu.SemaphoreType.DMA
     scratch = [
+        pltpu.SMEM(block_pos.shape, jnp.int32),
+        pltpu.VMEM((tokens, lat), bf16),
+        pltpu.VMEM((ROPE, tokens), bf16),
+        pltpu.VMEM((tokens, heads * ROPE), bf16),
         pltpu.VMEM((SPAN, 2, 64, WIDE), bf16),
         pltpu.VMEM((rows, WIDE), bf16),
         pltpu.VMEM((rows, lat), bf16),
@@ -295,7 +301,6 @@
         *[pltpu.VMEM((keys, CHUNK), f32) for _ in range(4)],
         pltpu.VMEM((keys, rows), bf16),
         pltpu.VMEM((keys, rows), bf16),
-        pltpu.VMEM((rows, lat), bf16),
         *pairs((2 * SPAN, 2, 32), f32),
         *pairs((2 * SPAN, 32), bf16),
         *pairs((2 * SPAN, 32), bf16),
@@ -303,7 +308,7 @@
         *pairs((3, 2, 32), bf16),
         *pairs((32,), bf16),
         *pairs((32,), bf16),
-        dma((2,)), dma((rows // CHUNK,)),
+        dma((6,)),
         dma((3,)), dma((3,)), dma((3,)), dma((3,)),
         dma((2,)), dma((2,)), dma((2, 3)), dma((2, 3)), dma((2,)), dma((2,)),
     ]
@@ -311,24 +316,32 @@
     dq, dqr, dkv, dkr = pl.pallas_call(
         functools.partial(kernel, n_ctx, heads),
         out_shape=(
-            jax.ShapeDtypeStruct((rows, lat), bf16),
-            jax.ShapeDtypeStruct((tokens, heads * ROPE), bf16),
-            jax.ShapeDtypeStruct((tokens // 4, lat), bf16),
-            jax.ShapeDtypeStruct((tokens // 4, ROPE), bf16),
+            pltpu.VMEM((rows, lat), bf16),
+            pltpu.VMEM((tokens, heads * ROPE), bf16),
+            pltpu.VMEM((tokens // 4, lat), bf16),
+            pltpu.VMEM((tokens // 4, ROPE), bf16),
         ),
-        in_specs=[smem, vmem, vmem, vmem, hbm, hbm],
-        out_specs=(hbm, vmem, vmem, vmem),
+        in_specs=[hbm] * 6,
+        out_specs=(vmem,) * 4,
         scratch_shapes=scratch,
         compiler_params=pltpu.CompilerParams(
-            collective_id=0, has_side_effects=True, vmem_limit_bytes=48 * 2**20
+            collective_id=0, has_side_effects=True, vmem_limit_bytes=56 * 2**20
         ),
         cost_estimate=pl.CostEstimate(
             flops=2 * macs, bytes_accessed=7 * 2**20, transcendentals=rows * keys
         ),
     )(
-        block_pos, kv_latent, k_rope, q_rope,
+        block_pos, kv_latent, k_rope.T, q_rope,
         q_latent.reshape(rows, lat), out_grad.reshape(rows, lat),
     )
+    results = (dq, dqr, dkv, dkr)
+    dq, dqr, dkv, dkr = pl.pallas_call(
+        move,
+        out_shape=tuple(jax.ShapeDtypeStruct(r.shape, r.dtype) for r in results),
+        in_specs=[vmem] * 4,
+        out_specs=(hbm,) * 4,
+        scratch_shapes=[dma((4,))],
+    )(*results)
     return dq.reshape(tokens, heads, lat), dqr, dkv, dkr
 
 

time: 49.1 us -> 45.5 us (0.927)
  local copies, waits for them, and re-layouts: 8.16 us -> 3.24 us
  Pallas kernels: 40 us -> 41.5 us
    unnamed x13 -> x8, local copies, waits for them, and re-layouts: 8.16 us -> 3.24 us
    pallas_call x1 -> x2, Pallas kernels: 40 us -> 41.5 us  [the longest x1 38.4 us: per_device(): pl.pallas_call(functools.partial(kernel, n_ctx, heads), out_shape=(pltpu....]
where the time goes in v1:
time: 45.5 us; the launch traced here: 45.4 us
  Pallas kernels  41.5 us (91%)
  local copies, waits for them, and re-layouts  3.24 us (7%)
  between operations  0.65 us (1%)
    pallas_call x1, Pallas kernels, per_device(): pl.pallas_call(functools.partial(kernel, n_ctx, heads), out_shape=(pltpu....  38.4 us
    unnamed x8, local copies, waits for them, and re-layouts  3.24 us
    pallas_call x1, Pallas kernels, per_device(): pl.pallas_call(move, out_shape=tuple((jax.ShapeDtypeStruct(r.shape, r.dty...  3.12 us

profile of v1, /device:TPU:1, one launch (start us, length us, event | category | flops | bytes accessed | tf_op | source)
XLA Modules:
  0.0 45.4 jit_solution(18190996788882855819)
XLA Ops:
  0.6 38.4 %shard_map.93 = (bf16[2048,512]{1,0:T(8,128)(2,1)S(1)}, bf16[128,1024]{1,0:T(8,128)(2,1)S(1)}, bf16[32,512]{1,0:T(8,128)(2,1)S(1)}, bf16[32,64]{1,0:T(8,128)(2,1)S(1)}) custom-call(s32[128]{0:T(128)} %pos_hbm.1, bf16[128,512]{1,0:T(8,128)(2,1)} %kv_hbm.1, bf16[64,128]{1,0:T(8,128)(2,1)} %bitcast.7, bf16[128,1024]{1,0:T(8,128)(2,1)} %qr_hbm.1, ...), custom_call_target="tpu_custom_call" | custom-call | flops 6174015488 | bytes 7340032 | tf_op jit(solution)/shard_map/pallas_call | solution.py:316
  39.0 0.0 copy-start
  39.0 1.3 %copy-done = bf16[2048,512]{1,0:T(8,128)(2,1)} copy-done((bf16[2048,512]{1,0:T(8,128)(2,1)}, bf16[2048,512]{1,0:T(8,128)(2,1)S(1)}, u32[]{:S(2)}) %copy-start) | copy-done | bytes 2097176
  40.4 0.0 copy-start.1
  40.4 0.7 %copy-done.1 = bf16[128,1024]{1,0:T(8,128)(2,1)} copy-done((bf16[128,1024]{1,0:T(8,128)(2,1)}, bf16[128,1024]{1,0:T(8,128)(2,1)S(1)}, u32[]{:S(2)}) %copy-start.1) | copy-done | bytes 262168
  41.1 0.0 copy-start.2
  41.1 0.6 %copy-done.2 = bf16[32,512]{1,0:T(8,128)(2,1)} copy-done((bf16[32,512]{1,0:T(8,128)(2,1)}, bf16[32,512]{1,0:T(8,128)(2,1)S(1)}, u32[]{:S(2)}) %copy-start.2) | copy-done | bytes 32792
  41.7 0.0 copy-start.3
  41.7 0.6 %copy-done.3 = bf16[32,64]{1,0:T(8,128)(2,1)} copy-done((bf16[32,64]{1,0:T(8,128)(2,1)}, bf16[32,64]{1,0:T(8,128)(2,1)S(1)}, u32[]{:S(2)}) %copy-start.3) | copy-done | bytes 4120
  42.3 3.1 %shard_map.94 = (bf16[2048,512]{1,0:T(8,128)(2,1)}, bf16[128,1024]{1,0:T(8,128)(2,1)}, bf16[32,512]{1,0:T(8,128)(2,1)}, bf16[32,64]{1,0:T(8,128)(2,1)}) custom-call(bf16[2048,512]{1,0:T(8,128)(2,1)} %copy-done, bf16[128,1024]{1,0:T(8,128)(2,1)} %copy-done.1, bf16[32,512]{1,0:T(8,128)(2,1)} %copy-done.2, bf16[32,64]{1,0:T(8,128)(2,1)} %copy-done.3), custom_call_target="tpu_custom_call" | custom-call | tf_op jit(solution)/shard_map/pallas_call | solution.py:338
Async XLA Ops:
  39.0 1.3 %copy-start = (bf16[2048,512]{1,0:T(8,128)(2,1)}, bf16[2048,512]{1,0:T(8,128)(2,1)S(1)}, u32[]{:S(2)}) copy-start(bf16[2048,512]{1,0:T(8,128)(2,1)S(1)} %get-tuple-element.12.refs_0_) | copy-start | bytes 6291460
  40.4 0.7 %copy-start.1 = (bf16[128,1024]{1,0:T(8,128)(2,1)}, bf16[128,1024]{1,0:T(8,128)(2,1)S(1)}, u32[]{:S(2)}) copy-start(bf16[128,1024]{1,0:T(8,128)(2,1)S(1)} %get-tuple-element.13.refs_1_) | copy-start | bytes 786436
  41.1 0.6 %copy-start.2 = (bf16[32,512]{1,0:T(8,128)(2,1)}, bf16[32,512]{1,0:T(8,128)(2,1)S(1)}, u32[]{:S(2)}) copy-start(bf16[32,512]{1,0:T(8,128)(2,1)S(1)} %get-tuple-element.14.refs_2_) | copy-start | bytes 98308
  41.7 0.6 %copy-start.3 = (bf16[32,64]{1,0:T(8,128)(2,1)}, bf16[32,64]{1,0:T(8,128)(2,1)S(1)}, u32[]{:S(2)}) copy-start(bf16[32,64]{1,0:T(8,128)(2,1)S(1)} %get-tuple-element.15.refs_3_) | copy-start | bytes 12292

commit v2 on v1

v2 whole, which is shorter than its diff:
```python
import functools

import jax
import jax.numpy as jnp
from jax import lax
from jax.experimental import pallas as pl
from jax.experimental.pallas import tpu as pltpu
from jax.sharding import PartitionSpec as P

SPAN = 4
LAT = 512
ROPE = 64
WIDE = 640
SCALE = 192.0 ** (-0.5)
SCALE_LOG2 = SCALE * 1.4426950408889634
CHUNK = 256
ORDER = (0, 1, 3, 2)
PLACE = tuple(ORDER.index(k) for k in range(SPAN))
GROUPS = ((0, 1), (1, 2), (3, 1))
SPLITS = ((0, 256), (256, 256), (512, 128))

NT = (((1,), (1,)), ((), ()))
TN = (((0,), (0,)), ((), ()))


def dot(a, b, dims=(((1,), (0,)), ((), ()))):
    return lax.dot_general(a, b, dims, preferred_element_type=jnp.float32)


def kernel(
    n_ctx, heads,
    pos_hbm, kv_hbm, kr_hbm, qr_hbm, q_hbm, g_hbm,
    dq_ref, dqr_ref, dkv_ref, dkr_ref,
    block_pos, kv_ref, kr_ref, qr_ref, kvr, qv, gv, rot32, s_a, s_b, e_buf, dp_buf, tops, sums, ds_t, w_t,
    *rest,
):
    parts = len(SPLITS)
    d, asb, arb, ysb, yrb, bsb, brb, csb, crb = [
        rest[i * parts:(i + 1) * parts] for i in range(9)
    ]
    (
        in_sem, f_send, f_recv, p_send, p_recv,
        a_send, a_recv, y_send, y_recv, b_send, b_recv, c_send, c_recv,
    ) = rest[9 * parts:]
    c = lax.axis_index("ctx")
    h = lax.axis_index("head")
    z = lax.div(h, 2)
    a = lax.rem(h, 2)
    sib = z * 2 + (1 - a)
    zpart = (1 - z) * 2 + a
    rows = qv.shape[0]
    half = rows // 2
    s_bufs = (s_a, s_b)

    def ctx_at(k):
        return lax.rem(c + k + n_ctx, n_ctx)

    load_keys = [
        pltpu.make_async_copy(kv_hbm, kv_ref, in_sem.at[0]),
        pltpu.make_async_copy(kr_hbm, kr_ref, in_sem.at[1]),
    ]
    load_rot = pltpu.make_async_copy(qr_hbm, qr_ref, in_sem.at[2])
    loads = [
        pltpu.make_async_copy(pos_hbm, block_pos, in_sem.at[3]),
        pltpu.make_async_copy(q_hbm, qv.at[:, pl.ds(0, LAT)], in_sem.at[4]),
        pltpu.make_async_copy(g_hbm, gv, in_sem.at[5]),
    ]
    for load in load_keys:
        load.start()

    barrier = pltpu.get_barrier_semaphore()
    peers = [(ctx_at(k), h) for k in (1, 3, -1, -3)] + [(c, sib), (c, zpart)]
    for peer in peers:
        pl.semaphore_signal(barrier, inc=1, device_id=peer, device_id_type=pl.DeviceIdType.MESH)

    for load in [load_rot, *loads]:
        load.start()

    for load in load_keys:
        load.wait()
    kvr[0, :, :, :, pl.ds(0, LAT)] = kv_ref[...].reshape(2, 2, 32, LAT)
    rot = kr_ref[...].astype(jnp.float32)
    kvr[0, :, :, :, pl.ds(LAT, 128)] = jnp.concatenate(
        [rot, jnp.zeros_like(rot)], axis=0
    ).T.astype(jnp.bfloat16).reshape(2, 2, 32, 128)

    pl.semaphore_wait(barrier, len(peers))

    def remote(src, dst, send, recv, peer):
        return pltpu.make_async_remote_copy(
            src_ref=src, dst_ref=dst, send_sem=send, recv_sem=recv,
            device_id=peer, device_id_type=pl.DeviceIdType.MESH,
        )

    flights = []
    arrived = {}

    def key_copy(index, source, target, peer):
        copy = remote(kvr.at[source], kvr.at[target], f_send.at[index], f_recv.at[index], peer)
        copy.start()
        flights.append(copy)
        return copy

    for index, (k, piece) in enumerate(((1, 0), (3, 1), (1, 1), (3, 0))):
        arrived[k, piece] = key_copy(
            index, (0, a, piece), (PLACE[k], a, piece), (ctx_at(k), h)
        )

    def relay():
        arrived[1, 0].wait_recv()
        arrived[2, 0] = key_copy(4, (PLACE[1], a, 0), (PLACE[2], a, 0), (ctx_at(1), h))
        arrived[3, 1].wait_recv()
        arrived[2, 1] = key_copy(5, (PLACE[3], a, 1), (PLACE[2], a, 1), (ctx_at(-1), h))

    load_rot.wait()
    tokens = qr_ref.shape[0]
    low = lax.broadcasted_iota(jnp.int32, (tokens, 128), 1) < ROPE
    for j in range(heads // 2):
        tile = qr_ref[:, pl.ds(j * 128, 128)].astype(jnp.float32)
        rot32[pl.ds(2 * j, tokens, stride=heads), :] = jnp.where(low, tile, 0.0)
        rot32[pl.ds(2 * j + 1, tokens, stride=heads), :] = jnp.where(
            low, pltpu.roll(tile, 64, 1), 0.0
        )
    qv[:, pl.ds(LAT, 128)] = rot32[...].astype(jnp.bfloat16)

    for load in loads:
        load.wait()
    passed = {}

    def pass_on(k):
        for piece in (0, 1):
            if (k, piece) not in ((1, 0), (3, 1)):
                arrived[k, piece].wait_recv()
        passed[k] = remote(
            kvr.at[PLACE[k], a], kvr.at[PLACE[k], a], p_send.at[k - 1], p_recv.at[k - 1], (c, sib)
        )
        passed[k].start()

    key_pos = [
        block_pos[2 * ctx_at(-ORDER[slot // 2]) + slot % 2] for slot in range(2 * SPAN)
    ]
    query_pos = [block_pos[2 * c], block_pos[2 * c + 1]]
    lane_row = lax.broadcasted_iota(jnp.int32, (64, CHUNK), 1)
    sub_row = lax.broadcasted_iota(jnp.int32, (64, CHUNK), 0)
    chunks = rows // CHUNK

    def score(group, i):
        first, count = GROUPS[group]
        at = pl.ds(i * CHUNK, CHUNK)
        keys = kvr[pl.ds(first, count)].reshape(count * 128, WIDE)
        s_buf = s_bufs[i % 2]
        s_buf[pl.ds(0, count * 128), :] = dot(keys, qv[at, :], NT)
        dp_buf[pl.ds(first * 128, count * 128), at] = dot(keys[:, :LAT], gv[at, :], NT)

    def soften(group, i):
        first, count = GROUPS[group]
        at = pl.ds(i * CHUNK, CHUNK)
        s_buf = s_bufs[i % 2]
        second = i * CHUNK // half
        ahead = lax.div(lane_row + (i * CHUNK - second * half), heads) - sub_row
        top = jnp.full((1, CHUNK), -1e30, jnp.float32)
        for j in range(2 * count):
            part = pl.ds(j * 64, 64)
            seen = ahead >= (key_pos[2 * first + j] - query_pos[second]) * 64
            s = jnp.where(seen, s_buf[part, :], -jnp.inf)
            s_buf[part, :] = s
            top = jnp.maximum(top, jnp.max(s, axis=0, keepdims=True))
        total = jnp.zeros((1, CHUNK), jnp.float32)
        for j in range(2 * count):
            e = jnp.exp2((s_buf[pl.ds(j * 64, 64), :] - top) * SCALE_LOG2)
            e_buf[pl.ds(first * 128 + j * 64, 64), at] = e
            total = total + jnp.sum(e, axis=0, keepdims=True)
        tops[pl.ds(group, 1), at] = top
        sums[pl.ds(group, 1), at] = total

    def join(i):
        at = pl.ds(i * CHUNK, CHUNK)
        parts = range(len(GROUPS))
        top_of = [tops[pl.ds(g, 1), at] for g in parts]
        top = functools.reduce(jnp.maximum, top_of)
        part_of = [jnp.exp2((t - top) * SCALE_LOG2) for t in top_of]
        total = sum(f * sums[pl.ds(g, 1), at] for g, f in zip(parts, part_of))
        inv = 1.0 / total
        factor = []
        for g in parts:
            factor += [part_of[g] * inv] * (2 * GROUPS[g][1])
        delta = jnp.zeros((1, CHUNK), jnp.float32)
        for slot in range(2 * SPAN):
            part = pl.ds(slot * 64, 64)
            w = (e_buf[part, at] * factor[slot]).astype(jnp.bfloat16)
            w_t[part, at] = w
            delta = delta + jnp.sum(
                w.astype(jnp.float32) * dp_buf[part, at], axis=0, keepdims=True
            )
        for slot in range(2 * SPAN):
            part = pl.ds(slot * 64, 64)
            ds_t[part, at] = (
                (e_buf[part, at] * factor[slot]) * (dp_buf[part, at] - delta)
            ).astype(jnp.bfloat16)

    score(0, 0)
    for i in range(chunks):
        if i == 2:
            relay()
        if i == 5:
            pass_on(1)
            pass_on(3)
        if i + 1 < chunks:
            score(0, i + 1)
        soften(0, i)
    passed[1].wait_recv()
    passed[3].wait_recv()
    score(1, 0)
    for i in range(chunks):
        if i == 4:
            pass_on(2)
        if i + 1 < chunks:
            score(1, i + 1)
        soften(1, i)
    passed[2].wait_recv()
    score(2, 0)
    for i in range(chunks):
        if i + 1 < chunks:
            score(2, i + 1)
        soften(2, i)
        join(i)


    def key_grads(n):
        first, width = SPLITS[n]
        part = SCALE * dot(ds_t[...], qv[:, pl.ds(first, width)])
        if first < LAT:
            part = part + dot(w_t[...], gv[:, pl.ds(first, width)])
        d[n][...] = part.reshape(2 * SPAN, 2, 32, width)
        asb[n][...] = d[n][:, pl.ds(1 - a, 1)].reshape(2 * SPAN, 32, width).astype(jnp.bfloat16)
        copy = remote(asb[n], arb[n], a_send.at[n], a_recv.at[n], (c, sib))
        copy.start()
        flights.append(copy)
        return copy

    def own(n, k, piece=None):
        width = SPLITS[n][1]
        if piece is None:
            return d[n][pl.ds(2 * PLACE[k], 2), pl.ds(a, 1)].reshape(2, 32, width)
        return d[n][pl.ds(2 * PLACE[k] + piece, 1), pl.ds(a, 1)].reshape(32, width)

    def sum_to(n, k, piece):
        index = k - 1 + piece
        copy = remote(
            bsb[n].at[index], brb[n].at[index], b_send.at[n, index], b_recv.at[n, index],
            (ctx_at(-k), h),
        )
        copy.start()
        flights.append(copy)
        return copy

    def add_cores(n, copy):
        copy.wait_recv()
        width = SPLITS[n][1]
        for k in (2, 1, 3, 0):
            got = arb[n][pl.ds(2 * PLACE[k], 2)].astype(jnp.float32)
            added = own(n, k) + got
            if k == 2:
                ysb[n][...] = added.astype(jnp.bfloat16)
                onward = []
                for piece, step in ((0, -1), (1, 1)):
                    onward.append(remote(
                        ysb[n].at[piece], yrb[n].at[piece], y_send.at[n, piece],
                        y_recv.at[n, piece], (ctx_at(step), h),
                    ))
                    onward[-1].start()
                    flights.append(onward[-1])
            else:
                d[n][pl.ds(2 * PLACE[k], 2), pl.ds(a, 1)] = added.reshape(2, 1, 32, width)
            if k == 1:
                bsb[n][1] = added[1].astype(jnp.bfloat16)
                sent = [sum_to(n, 1, 1)]
            if k == 3:
                bsb[n][2] = added[0].astype(jnp.bfloat16)
                sent.append(sum_to(n, 3, 0))
        return onward, sent

    def merge(n, onward, sent):
        for copy, (k, piece) in zip(onward, ((1, 0), (3, 1))):
            copy.wait_recv()
            added = own(n, k, piece) + yrb[n][piece].astype(jnp.float32)
            bsb[n][k - 1 + piece] = added.astype(jnp.bfloat16)
            sent.append(sum_to(n, k, piece))
        return sent

    def add_context(n, sent):
        for copy in sent:
            copy.wait_recv()
        width = SPLITS[n][1]
        near = brb[n][pl.ds(0, 2)].astype(jnp.float32)
        far = brb[n][pl.ds(2, 2)].astype(jnp.float32)
        d[n][pl.ds(0, 2), pl.ds(a, 1)] = (own(n, 0) + near + far).reshape(2, 1, 32, width)
        csb[n][...] = d[n][pl.ds(1 - z, 1), pl.ds(a, 1)].reshape(32, width).astype(jnp.bfloat16)
        copy = remote(csb[n], crb[n], c_send.at[n], c_recv.at[n], (c, zpart))
        copy.start()
        flights.append(copy)
        return copy

    def finish(n, copy):
        copy.wait_recv()
        first, width = SPLITS[n]
        result = d[n][pl.ds(z, 1), pl.ds(a, 1)].reshape(32, width) + crb[n][...].astype(jnp.float32)
        result = result.astype(jnp.bfloat16)
        if first < LAT:
            dkv_ref[:, pl.ds(first, width)] = result
        else:
            dkr_ref[...] = result[:, :ROPE]

    def query_grads(i):
        start = i * CHUNK
        at = pl.ds(start, CHUNK)
        keys = kvr[...].reshape(SPAN * 128, WIDE)
        grad = SCALE * dot(ds_t[:, at], keys, TN)
        dq_ref[at, :] = grad[:, :LAT].astype(jnp.bfloat16)
        rot32[at, :] = grad[:, LAT:]

    a0 = key_grads(0)
    a1 = key_grads(1)
    y0 = add_cores(0, a0)
    a2 = key_grads(2)
    query_grads(0)
    y1 = add_cores(1, a1)
    query_grads(1)
    b0 = merge(0, *y0)
    y2 = add_cores(2, a2)
    query_grads(2)
    b1 = merge(1, *y1)
    query_grads(3)
    c0 = add_context(0, b0)
    b2 = merge(2, *y2)
    query_grads(4)
    c1 = add_context(1, b1)
    query_grads(5)
    query_grads(6)
    query_grads(7)

    for j in range(heads // 2):
        even = rot32[pl.ds(2 * j, tokens, stride=heads), :]
        odd = rot32[pl.ds(2 * j + 1, tokens, stride=heads), :]
        dqr_ref[:, pl.ds(j * 128, 128)] = jnp.where(
            low, even, pltpu.roll(odd, 64, 1)
        ).astype(jnp.bfloat16)

    c2 = add_context(2, b2)
    finish(0, c0)
    finish(1, c1)
    for copy in [*passed.values(), *flights]:
        copy.wait_send()
    finish(2, c2)


def move(*refs):
    sources, targets, sem = refs[:4], refs[4:8], refs[8]
    copies = [
        pltpu.make_async_copy(s, t, sem.at[i]) for i, (s, t) in enumerate(zip(sources, targets))
    ]
    for copy in copies:
        copy.start()
    for copy in copies:
        copy.wait()


def per_device(q_latent, q_rope, kv_latent, k_rope, out_grad, block_pos):
    tokens, heads, lat = q_latent.shape
    rows = tokens * heads
    keys = SPAN * tokens
    n_ctx = lax.axis_size("ctx")
    bf16, f32 = jnp.bfloat16, jnp.float32
    vmem = pl.BlockSpec(memory_space=pltpu.VMEM)
    hbm = pl.BlockSpec(memory_space=pltpu.HBM)
    widths = [width for _, width in SPLITS]
    n = len(SPLITS)

    def pairs(shape, kind):
        return [pltpu.VMEM(shape + (width,), kind) for width in widths]

    dma = pltpu.SemaphoreType.DMA
    scratch = [
        pltpu.SMEM(block_pos.shape, jnp.int32),
        pltpu.VMEM((tokens, lat), bf16),
        pltpu.VMEM((ROPE, tokens), bf16),
        pltpu.VMEM((tokens, heads * ROPE), bf16),
        pltpu.VMEM((SPAN, 2, 2, 32, WIDE), bf16),
        pltpu.VMEM((rows, WIDE), bf16),
        pltpu.VMEM((rows, lat), bf16),
        pltpu.VMEM((rows, 128), f32),
        *[pltpu.VMEM((keys // 2, CHUNK), f32) for _ in range(2)],
        *[pltpu.VMEM((keys, rows), f32) for _ in range(2)],
        *[pltpu.VMEM((8, rows), f32) for _ in range(2)],
        pltpu.VMEM((keys, rows), bf16),
        pltpu.VMEM((keys, rows), bf16),
        *pairs((2 * SPAN, 2, 32), f32),
        *pairs((2 * SPAN, 32), bf16),
        *pairs((2 * SPAN, 32), bf16),
        *pairs((2, 32), bf16),
        *pairs((2, 32), bf16),
        *pairs((4, 32), bf16),
        *pairs((4, 32), bf16),
        *pairs((32,), bf16),
        *pairs((32,), bf16),
        dma((6,)), dma((6,)), dma((6,)), dma((3,)), dma((3,)),
        dma((n,)), dma((n,)), dma((n, 2)), dma((n, 2)), dma((n, 4)), dma((n, 4)),
        dma((n,)), dma((n,)),
    ]
    macs = rows * keys * (WIDE * 3 + 2 * lat)
    dq, dqr, dkv, dkr = pl.pallas_call(
        functools.partial(kernel, n_ctx, heads),
        out_shape=(
            pltpu.VMEM((rows, lat), bf16),
            pltpu.VMEM((tokens, heads * ROPE), bf16),
            pltpu.VMEM((tokens // 4, lat), bf16),
            pltpu.VMEM((tokens // 4, ROPE), bf16),
        ),
        in_specs=[hbm] * 6,
        out_specs=(vmem,) * 4,
        scratch_shapes=scratch,
        compiler_params=pltpu.CompilerParams(
            collective_id=0, has_side_effects=True, vmem_limit_bytes=56 * 2**20
        ),
        cost_estimate=pl.CostEstimate(
            flops=2 * macs, bytes_accessed=7 * 2**20, transcendentals=rows * keys
        ),
    )(
        block_pos, kv_latent, k_rope.T, q_rope,
        q_latent.reshape(rows, lat), out_grad.reshape(rows, lat),
    )
    results = (dq, dqr, dkv, dkr)
    dq, dqr, dkv, dkr = pl.pallas_call(
        move,
        out_shape=tuple(jax.ShapeDtypeStruct(r.shape, r.dtype) for r in results),
        in_specs=[vmem] * 4,
        out_specs=(hbm,) * 4,
        scratch_shapes=[dma((4,))],
        compiler_params=pltpu.CompilerParams(vmem_limit_bytes=2**20),
    )(*results)
    return dq.reshape(tokens, heads, lat), dqr, dkv, dkr


def solution(mesh):
    in_specs = (
        P("ctx", "head", None),
        P("ctx", "head"),
        P("ctx", None),
        P("ctx", None),
        P("ctx", "head", None),
        P(),
    )
    out_specs = (
        P("ctx", "head", None),
        P("ctx", "head"),
        P(("ctx", "head"), None),
        P(("ctx", "head"), None),
    )
    return jax.shard_map(
        per_device, mesh=mesh, in_specs=in_specs, out_specs=out_specs, check_vma=False
    )
```

time: 45.5 us -> 44.2 us (0.971)
  the two profiles are of different devices: /device:TPU:1 before, /device:TPU:120 now
where the time goes in v2:
time: 44.2 us; the launch traced here: 44.1 us
  Pallas kernels  43.5 us (98%)
  between operations  0.64 us (1%)
    pallas_call x1, Pallas kernels, per_device(): pl.pallas_call(functools.partial(kernel, n_ctx, heads), out_shape=(pltpu....  42.1 us
    pallas_call x1, Pallas kernels, per_device(): pl.pallas_call(move, out_shape=tuple((jax.ShapeDtypeStruct(r.shape, r.dty...  1.43 us

profile of v2, /device:TPU:120, one launch (start us, length us, event | category | flops | bytes accessed | tf_op | source)
XLA Modules:
  0.0 44.1 jit_solution(14863447138298800102)
XLA Ops:
  0.6 42.1 %shard_map.93 = (bf16[2048,512]{1,0:T(8,128)(2,1)S(1)}, bf16[128,1024]{1,0:T(8,128)(2,1)S(1)}, bf16[32,512]{1,0:T(8,128)(2,1)S(1)}, bf16[32,64]{1,0:T(8,128)(2,1)S(1)}) custom-call(s32[128]{0:T(128)} %pos_hbm.1, bf16[128,512]{1,0:T(8,128)(2,1)} %kv_hbm.1, bf16[64,128]{1,0:T(8,128)(2,1)} %bitcast.7, bf16[128,1024]{1,0:T(8,128)(2,1)} %qr_hbm.1, ...), custom_call_target="tpu_custom_call" | custom-call | flops 6174015488 | bytes 7340032 | tf_op jit(solution)/shard_map/pallas_call | solution.py:411
  42.7 1.4 %shard_map.94 = (bf16[2048,512]{1,0:T(8,128)(2,1)}, bf16[128,1024]{1,0:T(8,128)(2,1)}, bf16[32,512]{1,0:T(8,128)(2,1)}, bf16[32,64]{1,0:T(8,128)(2,1)}) custom-call(bf16[2048,512]{1,0:T(8,128)(2,1)S(1)} %get-tuple-element.12.refs_0_, bf16[128,1024]{1,0:T(8,128)(2,1)S(1)} %get-tuple-element.13.refs_1_, bf16[32,512]{1,0:T(8,128)(2,1)S(1)} %get-tuple-element.14.refs_2_, ...), custom_call_target="tpu_custom_call" | custom-call | tf_op jit(solution)/shard_map/pallas_call | solution.py:433

commit v3 on v1

--- a/solution.py
+++ b/solution.py
@@ -14,7 +14,12 @@
 SCALE = 192.0 ** (-0.5)
 SCALE_LOG2 = SCALE * 1.4426950408889634
 CHUNK = 256
+ORDER = (0, 1, 3, 2)
+PLACE = tuple(ORDER.index(k) for k in range(SPAN))
+GROUPS = ((0, 1), (1, 2), (3, 1))
 SPLITS = ((256, 384), (0, 256))
+
+PIECES = 8
 
 NT = (((1,), (1,)), ((), ()))
 TN = (((0,), (0,)), ((), ()))
@@ -28,7 +33,7 @@
     n_ctx, heads,
     pos_hbm, kv_hbm, kr_hbm, qr_hbm, q_hbm, g_hbm,
     dq_ref, dqr_ref, dkv_ref, dkr_ref,
-    block_pos, kv_ref, kr_ref, qr_ref, kvr, qv, gv, rot32, s_a, s_b, dp_a, dp_b, ds_t, w_t,
+    block_pos, kv_ref, kr_ref, qr_ref, kvr, qv, gv, rot32, s_a, s_b, e_buf, dp_buf, tops, sums, ds_t, w_t,
     d0, d1, as0, as1, ar0, ar1, bs0, bs1, br0, br1, cs0, cs1, cr0, cr1,
     in_sem, f_send, f_recv, p_send, p_recv,
     a_send, a_recv, b_send, b_recv, c_send, c_recv,
@@ -41,6 +46,7 @@
     zpart = (1 - z) * 2 + a
     rows = qv.shape[0]
     half = rows // 2
+    s_bufs = (s_a, s_b)
 
     def ctx_at(k):
         return lax.rem(c + k + n_ctx, n_ctx)
@@ -55,13 +61,16 @@
         pltpu.make_async_copy(q_hbm, qv.at[:, pl.ds(0, LAT)], in_sem.at[4]),
         pltpu.make_async_copy(g_hbm, gv, in_sem.at[5]),
     ]
-    for load in [*load_keys, load_rot, *loads]:
+    for load in load_keys:
         load.start()
 
     barrier = pltpu.get_barrier_semaphore()
     peers = [(ctx_at(k), h) for k in (1, 2, 3, -1, -2, -3)] + [(c, sib), (c, zpart)]
     for peer in peers:
         pl.semaphore_signal(barrier, inc=1, device_id=peer, device_id_type=pl.DeviceIdType.MESH)
+
+    for load in [load_rot, *loads]:
+        load.start()
 
     for load in load_keys:
         load.wait()
@@ -80,9 +89,9 @@
         )
 
     forward = {}
-    for k in (2, 1, 3):
+    for k in (1, 3, 2):
         forward[k] = remote(
-            kvr.at[0, a], kvr.at[k, a], f_send.at[k - 1], f_recv.at[k - 1], (ctx_at(k), h)
+            kvr.at[0, a], kvr.at[PLACE[k], a], f_send.at[k - 1], f_recv.at[k - 1], (ctx_at(k), h)
         )
         forward[k].start()
 
@@ -97,105 +106,146 @@
         )
     qv[:, pl.ds(LAT, 128)] = rot32[...].astype(jnp.bfloat16)
 
+    for load in loads:
+        load.wait()
     passed = {}
-    for k in (1, 3, 2):
+
+    def pass_on(k):
         forward[k].wait_recv()
         passed[k] = remote(
-            kvr.at[k, a], kvr.at[k, a], p_send.at[k - 1], p_recv.at[k - 1], (c, sib)
+            kvr.at[PLACE[k], a], kvr.at[PLACE[k], a], p_send.at[k - 1], p_recv.at[k - 1], (c, sib)
         )
         passed[k].start()
-    for load in loads:
-        load.wait()
-    for k in (1, 3, 2):
-        passed[k].wait_recv()
 
     key_pos = [
-        block_pos[2 * ctx_at(-(slot // 2)) + slot % 2] for slot in range(2 * SPAN)
+        block_pos[2 * ctx_at(-ORDER[slot // 2]) + slot % 2] for slot in range(2 * SPAN)
     ]
     query_pos = [block_pos[2 * c], block_pos[2 * c + 1]]
-
-    def score(start, s_buf, dp_buf):
-        at = pl.ds(start, CHUNK)
-        keys = kvr[...].reshape(SPAN * 128, WIDE)
-        s_buf[...] = dot(keys, qv[at, :], NT)
-        dp_buf[...] = dot(keys[:, :LAT], gv[at, :], NT)
-
     lane_row = lax.broadcasted_iota(jnp.int32, (64, CHUNK), 1)
     sub_row = lax.broadcasted_iota(jnp.int32, (64, CHUNK), 0)
-
-    def soften(start, s_buf, dp_buf):
-        at = pl.ds(start, CHUNK)
-        second = start // half
-        pos = query_pos[second] * 64
-        ahead = lax.div(lane_row + (start - second * half), heads) - sub_row
-        top = None
+    chunks = rows // CHUNK
+
+    def score(group, i):
+        first, count = GROUPS[group]
+        at = pl.ds(i * CHUNK, CHUNK)
+        keys = kvr[pl.ds(first, count)].reshape(count * 128, WIDE)
+        s_buf = s_bufs[i % 2]
+        s_buf[pl.ds(0, count * 128), :] = dot(keys, qv[at, :], NT)
+        dp_buf[pl.ds(first * 128, count * 128), at] = dot(keys[:, :LAT], gv[at, :], NT)
+
+    def soften(group, i):
+        first, count = GROUPS[group]
+        at = pl.ds(i * CHUNK, CHUNK)
+        s_buf = s_bufs[i % 2]
+        second = i * CHUNK // half
+        ahead = lax.div(lane_row + (i * CHUNK - second * half), heads) - sub_row
+        top = jnp.full((1, CHUNK), -1e30, jnp.float32)
+        hidden = []
+        for j in range(2 * count):
+            part = pl.ds(j * 64, 64)
+            s = s_buf[part, :]
+            if 2 * first + j == second:
+                s = jnp.where(ahead >= 0, s, -jnp.inf)
+                s_buf[part, :] = s
+                hidden.append(0.0)
+            else:
+                hidden.append(
+                    jnp.where(key_pos[2 * first + j] < query_pos[second], 0.0, jnp.inf)
+                )
+            top = jnp.maximum(top, jnp.max(s, axis=0, keepdims=True) - hidden[j])
+        total = jnp.zeros((1, CHUNK), jnp.float32)
+        for j in range(2 * count):
+            e = jnp.exp2((s_buf[pl.ds(j * 64, 64), :] - (top + hidden[j])) * SCALE_LOG2)
+            e_buf[pl.ds(first * 128 + j * 64, 64), at] = e
+            total = total + jnp.sum(e, axis=0, keepdims=True)
+        tops[pl.ds(group, 1), at] = top
+        sums[pl.ds(group, 1), at] = total
+
+    def join(i):
+        at = pl.ds(i * CHUNK, CHUNK)
+        parts = range(len(GROUPS))
+        top_of = [tops[pl.ds(g, 1), at] for g in parts]
+        top = functools.reduce(jnp.maximum, top_of)
+        part_of = [jnp.exp2((t - top) * SCALE_LOG2) for t in top_of]
+        total = sum(f * sums[pl.ds(g, 1), at] for g, f in zip(parts, part_of))
+        inv = 1.0 / total
+        factor = []
+        for g in parts:
+            factor += [part_of[g] * inv] * (2 * GROUPS[g][1])
+        delta = jnp.zeros((1, CHUNK), jnp.float32)
         for slot in range(2 * SPAN):
             part = pl.ds(slot * 64, 64)
-            seen = ahead >= key_pos[slot] * 64 - pos
-            s = jnp.where(seen, s_buf[part, :], -jnp.inf)
-            s_buf[part, :] = s
-            m = jnp.max(s, axis=0, keepdims=True)
-            top = m if top is None else jnp.maximum(top, m)
-        total = None
-        for slot in range(2 * SPAN):
-            part = pl.ds(slot * 64, 64)
-            e = jnp.exp2((s_buf[part, :] - top) * SCALE_LOG2)
-            s_buf[part, :] = e
-            t = jnp.sum(e, axis=0, keepdims=True)
-            total = t if total is None else total + t
-        inv = 1.0 / total
-        delta = None
-        for slot in range(2 * SPAN):
-            part = pl.ds(slot * 64, 64)
-            w = (s_buf[part, :] * inv).astype(jnp.bfloat16)
+            w = (e_buf[part, at] * factor[slot]).astype(jnp.bfloat16)
             w_t[part, at] = w
-            t = jnp.sum(w.astype(jnp.float32) * dp_buf[part, :], axis=0, keepdims=True)
-            delta = t if delta is None else delta + t
+            delta = delta + jnp.sum(
+                w.astype(jnp.float32) * dp_buf[part, at], axis=0, keepdims=True
+            )
         for slot in range(2 * SPAN):
             part = pl.ds(slot * 64, 64)
             ds_t[part, at] = (
-                (s_buf[part, :] * inv) * (dp_buf[part, :] - delta)
+                (e_buf[part, at] * factor[slot]) * (dp_buf[part, at] - delta)
             ).astype(jnp.bfloat16)
 
-    score(0, s_a, dp_a)
-
-    for start in range(0, rows, 2 * CHUNK):
-        score(start + CHUNK, s_b, dp_b)
-        soften(start, s_a, dp_a)
-        if start + 2 * CHUNK < rows:
-            score(start + 2 * CHUNK, s_a, dp_a)
-        soften(start + CHUNK, s_b, dp_b)
+    score(0, 0)
+    for i in range(chunks):
+        if i == 5:
+            pass_on(1)
+            pass_on(3)
+        if i + 1 < chunks:
+            score(0, i + 1)
+        soften(0, i)
+    passed[1].wait_recv()
+    passed[3].wait_recv()
+    score(1, 0)
+    for i in range(chunks):
+        if i == 4:
+            pass_on(2)
+        if i + 1 < chunks:
+            score(1, i + 1)
+        soften(1, i)
+    passed[2].wait_recv()
+    score(2, 0)
+    for i in range(chunks):
+        if i + 1 < chunks:
+            score(2, i + 1)
+        soften(2, i)
+        join(i)
 
     d, asb, arb, bsb, brb = (d0, d1), (as0, as1), (ar0, ar1), (bs0, bs1), (br0, br1)
     csb, crb = (cs0, cs1), (cr0, cr1)
 
-    def key_grads(n):
+    def key_grads(n, first_place, count):
         first, width = SPLITS[n]
-        shape = (2 * SPAN, 2, 32, width)
-        part = SCALE * dot(ds_t[...], qv[:, pl.ds(first, width)])
+        at = pl.ds(first_place * 128, count * 128)
+        slots = pl.ds(2 * first_place, 2 * count)
+        shape = (2 * count, 2, 32)
+        part = SCALE * dot(ds_t[at, :], qv[:, pl.ds(first, width)])
         latent = min(width, LAT - first)
-        other = dot(w_t[...], gv[:, pl.ds(first, latent)])
-        if latent == width:
-            d[n][...] = (part + other).reshape(shape)
-        else:
-            d[n][:, :, :, pl.ds(0, latent)] = (part[:, :latent] + other).reshape(shape[:3] + (latent,))
-            d[n][:, :, :, pl.ds(latent, width - latent)] = part[:, latent:].reshape(
-                shape[:3] + (width - latent,)
+        other = dot(w_t[at, :], gv[:, pl.ds(first, latent)])
+        d[n][slots, :, :, pl.ds(0, latent)] = (part[:, :latent] + other).reshape(shape + (latent,))
+        if latent < width:
+            d[n][slots, :, :, pl.ds(latent, width - latent)] = part[:, latent:].reshape(
+                shape + (width - latent,)
             )
-        asb[n][...] = d[n][:, pl.ds(1 - a, 1)].reshape(2 * SPAN, 32, width).astype(jnp.bfloat16)
-        copy = remote(asb[n], arb[n], a_send.at[n], a_recv.at[n], (c, sib))
+        asb[n][slots] = d[n][slots, pl.ds(1 - a, 1)].reshape(2 * count, 32, width).astype(
+            jnp.bfloat16
+        )
+        far = min(first_place, 1)
+        copy = remote(
+            asb[n].at[slots], arb[n].at[slots], a_send.at[n, far], a_recv.at[n, far], (c, sib)
+        )
         copy.start()
         return copy
 
     def own(n, k):
         width = SPLITS[n][1]
-        return d[n][pl.ds(2 * k, 2), pl.ds(a, 1)].reshape(2, 32, width)
+        return d[n][pl.ds(2 * PLACE[k], 2), pl.ds(a, 1)].reshape(2, 32, width)
 
     def add_cores(n, copy):
         copy.wait_recv()
         sends = []
         for k in (2, 1, 3):
-            got = arb[n][pl.ds(2 * k, 2)].astype(jnp.float32)
+            got = arb[n][pl.ds(2 * PLACE[k], 2)].astype(jnp.float32)
             bsb[n][k - 1] = (own(n, k) + got).astype(jnp.bfloat16)
             sends.append(remote(
                 bsb[n].at[k - 1], brb[n].at[k - 1], b_send.at[n, k - 1], b_recv.at[n, k - 1],
@@ -204,14 +254,14 @@
             sends[-1].start()
         return sends
 
-    def add_context(n, sends):
-        for copy in sends:
+    def add_context(n, near, sends):
+        for copy in [near, *sends]:
             copy.wait_recv()
-        sums = own(n, 0) + arb[n][pl.ds(0, 2)].astype(jnp.float32)
+        added = own(n, 0) + arb[n][pl.ds(0, 2)].astype(jnp.float32)
         for k in (1, 2, 3):
-            sums = sums + brb[n][k - 1].astype(jnp.float32)
+            added = added + brb[n][k - 1].astype(jnp.float32)
         width = SPLITS[n][1]
-        d[n][pl.ds(0, 2), pl.ds(a, 1)] = sums.reshape(2, 1, 32, width)
+        d[n][pl.ds(0, 2), pl.ds(a, 1)] = added.reshape(2, 1, 32, width)
         csb[n][...] = d[n][pl.ds(1 - z, 1), pl.ds(a, 1)].reshape(32, width).astype(jnp.bfloat16)
         copy = remote(csb[n], crb[n], c_send.at[n], c_recv.at[n], (c, zpart))
         copy.start()
@@ -235,19 +285,14 @@
         dq_ref[at, :] = grad[:, :LAT].astype(jnp.bfloat16)
         rot32[at, :] = grad[:, LAT:]
 
-    a0 = key_grads(0)
-    a1 = key_grads(1)
+    a0 = key_grads(0, 1, 3)
+    a1 = key_grads(1, 1, 3)
     b0 = add_cores(0, a0)
-    query_grads(0)
-    query_grads(1)
+    n0 = key_grads(0, 0, 1)
     b1 = add_cores(1, a1)
-    query_grads(2)
-    query_grads(3)
-    query_grads(4)
-    c0 = add_context(0, b0)
-    query_grads(5)
-    query_grads(6)
-    query_grads(7)
+    n1 = key_grads(1, 0, 1)
+    for i in range(chunks):
+        query_grads(i)
 
     for j in range(heads // 2):
         even = rot32[pl.ds(2 * j, tokens, stride=heads), :]
@@ -256,9 +301,10 @@
             low, even, pltpu.roll(odd, 64, 1)
         ).astype(jnp.bfloat16)
 
-    c1 = add_context(1, b1)
+    c0 = add_context(0, n0, b0)
+    c1 = add_context(1, n1, b1)
     finish(0, c0)
-    for copy in [*forward.values(), *passed.values(), a0, a1, *b0, *b1, c0]:
+    for copy in [*forward.values(), *passed.values(), a0, a1, n0, n1, *b0, *b1, c0]:
         copy.wait_send()
     finish(1, c1)
     c1.wait_send()
@@ -266,8 +312,15 @@
 
 def move(*refs):
     sources, targets, sem = refs[:4], refs[4:8], refs[8]
+    rows = sources[0].shape[0] // PIECES
     copies = [
-        pltpu.make_async_copy(s, t, sem.at[i]) for i, (s, t) in enumerate(zip(sources, targets))
+        pltpu.make_async_copy(
+            sources[0].at[pl.ds(i * rows, rows)], targets[0].at[pl.ds(i * rows, rows)], sem.at[i]
+        )
+        for i in range(PIECES)
+    ]
+    copies += [
+        pltpu.make_async_copy(sources[i], targets[i], sem.at[PIECES + i - 1]) for i in (1, 2, 3)
     ]
     for copy in copies:
         copy.start()
@@ -298,7 +351,9 @@
         pltpu.VMEM((rows, WIDE), bf16),
         pltpu.VMEM((rows, lat), bf16),
         pltpu.VMEM((rows, 128), f32),
-        *[pltpu.VMEM((keys, CHUNK), f32) for _ in range(4)],
+        *[pltpu.VMEM((keys // 2, CHUNK), f32) for _ in range(2)],
+        *[pltpu.VMEM((keys, rows), f32) for _ in range(2)],
+        *[pltpu.VMEM((8, rows), f32) for _ in range(2)],
         pltpu.VMEM((keys, rows), bf16),
         pltpu.VMEM((keys, rows), bf16),
         *pairs((2 * SPAN, 2, 32), f32),
@@ -310,7 +365,7 @@
         *pairs((32,), bf16),
         dma((6,)),
         dma((3,)), dma((3,)), dma((3,)), dma((3,)),
-        dma((2,)), dma((2,)), dma((2, 3)), dma((2, 3)), dma((2,)), dma((2,)),
+        dma((2, 2)), dma((2, 2)), dma((2, 3)), dma((2, 3)), dma((2,)), dma((2,)),
     ]
     macs = rows * keys * (WIDE * 3 + 2 * lat)
     dq, dqr, dkv, dkr = pl.pallas_call(
@@ -340,7 +395,8 @@
         out_shape=tuple(jax.ShapeDtypeStruct(r.shape, r.dtype) for r in results),
         in_specs=[vmem] * 4,
         out_specs=(hbm,) * 4,
-        scratch_shapes=[dma((4,))],
+        scratch_shapes=[dma((PIECES + 3,))],
+        compiler_params=pltpu.CompilerParams(vmem_limit_bytes=2**20),
     )(*results)
     return dq.reshape(tokens, heads, lat), dqr, dkv, dkr
 

time: 45.5 us -> 39.2 us (0.86)
  local copies, waits for them, and re-layouts: 3.24 us -> 0 us
  Pallas kernels: 41.5 us -> 38.5 us
    unnamed x8 -> x0, local copies, waits for them, and re-layouts: 3.24 us -> none
    pallas_call x1, Pallas kernels: 3.12 us -> 1.49 us  [per_device(): pl.pallas_call(move, out_shape=tuple((jax.ShapeDtypeStruct(r.shape, r.dty...]
    pallas_call x1, Pallas kernels: 38.4 us -> 37 us  [per_device(): pl.pallas_call(functools.partial(kernel, n_ctx, heads), out_shape=(pltpu....]
where the time goes in v3:
time: 39.2 us
  Pallas kernels  38.5 us (98%)
  between operations  0.64 us (2%)
    pallas_call x1, Pallas kernels, per_device(): pl.pallas_call(functools.partial(kernel, n_ctx, heads), out_shape=(pltpu....  37 us
    pallas_call x1, Pallas kernels, per_device(): pl.pallas_call(move, out_shape=tuple((jax.ShapeDtypeStruct(r.shape, r.dty...  1.49 us

profile of v3, /device:TPU:1, one launch (start us, length us, event | category | flops | bytes accessed | tf_op | source)
XLA Modules:
  0.0 39.2 jit_solution(2054791868960078874)
XLA Ops:
  0.6 37.0 %shard_map.93 = (bf16[2048,512]{1,0:T(8,128)(2,1)S(1)}, bf16[128,1024]{1,0:T(8,128)(2,1)S(1)}, bf16[32,512]{1,0:T(8,128)(2,1)S(1)}, bf16[32,64]{1,0:T(8,128)(2,1)S(1)}) custom-call(s32[128]{0:T(128)} %pos_hbm.1, bf16[128,512]{1,0:T(8,128)(2,1)} %kv_hbm.1, bf16[64,128]{1,0:T(8,128)(2,1)} %bitcast.7, bf16[128,1024]{1,0:T(8,128)(2,1)} %qr_hbm.1, ...), custom_call_target="tpu_custom_call" | custom-call | flops 6174015488 | bytes 7340032 | tf_op jit(solution)/shard_map/pallas_call | solution.py:371
  37.7 1.5 %shard_map.94 = (bf16[2048,512]{1,0:T(8,128)(2,1)}, bf16[128,1024]{1,0:T(8,128)(2,1)}, bf16[32,512]{1,0:T(8,128)(2,1)}, bf16[32,64]{1,0:T(8,128)(2,1)}) custom-call(bf16[2048,512]{1,0:T(8,128)(2,1)S(1)} %get-tuple-element.12.refs_0_, bf16[128,1024]{1,0:T(8,128)(2,1)S(1)} %get-tuple-element.13.refs_1_, bf16[32,512]{1,0:T(8,128)(2,1)S(1)} %get-tuple-element.14.refs_2_, ...), custom_call_target="tpu_custom_call" | custom-call | tf_op jit(solution)/shard_map/pallas_call | solution.py:393

commit v4 on v3

--- a/solution.py
+++ b/solution.py
@@ -17,7 +17,7 @@
 ORDER = (0, 1, 3, 2)
 PLACE = tuple(ORDER.index(k) for k in range(SPAN))
 GROUPS = ((0, 1), (1, 2), (3, 1))
-SPLITS = ((256, 384), (0, 256))
+SPLITS = ((0, 256), (256, 384))
 
 PIECES = 8
 
@@ -61,15 +61,12 @@
         pltpu.make_async_copy(q_hbm, qv.at[:, pl.ds(0, LAT)], in_sem.at[4]),
         pltpu.make_async_copy(g_hbm, gv, in_sem.at[5]),
     ]
-    for load in load_keys:
-        load.start()
-
     barrier = pltpu.get_barrier_semaphore()
-    peers = [(ctx_at(k), h) for k in (1, 2, 3, -1, -2, -3)] + [(c, sib), (c, zpart)]
+    peers = [(ctx_at(k), h) for k in (-3, -2, -1, 3, 2, 1)] + [(c, sib), (c, zpart)]
     for peer in peers:
         pl.semaphore_signal(barrier, inc=1, device_id=peer, device_id_type=pl.DeviceIdType.MESH)
 
-    for load in [load_rot, *loads]:
+    for load in [*load_keys, load_rot, *loads]:
         load.start()
 
     for load in load_keys:

time: 39.2 us -> 38.9 us (level)
  no operation moved by 1% of the time
where the time goes in v4:
time: 38.9 us; the launch traced here: 38.8 us
  Pallas kernels  38.2 us (98%)
  between operations  0.64 us (2%)
    pallas_call x1, Pallas kernels, per_device(): pl.pallas_call(functools.partial(kernel, n_ctx, heads), out_shape=(pltpu....  36.7 us
    pallas_call x1, Pallas kernels, per_device(): pl.pallas_call(move, out_shape=tuple((jax.ShapeDtypeStruct(r.shape, r.dty...  1.49 us

profile of v4, /device:TPU:1, one launch (start us, length us, event | category | flops | bytes accessed | tf_op | source)
XLA Modules:
  0.0 38.8 jit_solution(1649927703218879211)
XLA Ops:
  0.6 36.7 %shard_map.93 = (bf16[2048,512]{1,0:T(8,128)(2,1)S(1)}, bf16[128,1024]{1,0:T(8,128)(2,1)S(1)}, bf16[32,512]{1,0:T(8,128)(2,1)S(1)}, bf16[32,64]{1,0:T(8,128)(2,1)S(1)}) custom-call(s32[128]{0:T(128)} %pos_hbm.1, bf16[128,512]{1,0:T(8,128)(2,1)} %kv_hbm.1, bf16[64,128]{1,0:T(8,128)(2,1)} %bitcast.7, bf16[128,1024]{1,0:T(8,128)(2,1)} %qr_hbm.1, ...), custom_call_target="tpu_custom_call" | custom-call | flops 6174015488 | bytes 7340032 | tf_op jit(solution)/shard_map/pallas_call | solution.py:368
  37.3 1.5 %shard_map.94 = (bf16[2048,512]{1,0:T(8,128)(2,1)}, bf16[128,1024]{1,0:T(8,128)(2,1)}, bf16[32,512]{1,0:T(8,128)(2,1)}, bf16[32,64]{1,0:T(8,128)(2,1)}) custom-call(bf16[2048,512]{1,0:T(8,128)(2,1)S(1)} %get-tuple-element.12.refs_0_, bf16[128,1024]{1,0:T(8,128)(2,1)S(1)} %get-tuple-element.13.refs_1_, bf16[32,512]{1,0:T(8,128)(2,1)S(1)} %get-tuple-element.14.refs_2_, ...), custom_call_target="tpu_custom_call" | custom-call | tf_op jit(solution)/shard_map/pallas_call | solution.py:390

commit v5 on v4

--- a/solution.py
+++ b/solution.py
@@ -16,7 +16,7 @@
 CHUNK = 256
 ORDER = (0, 1, 3, 2)
 PLACE = tuple(ORDER.index(k) for k in range(SPAN))
-GROUPS = ((0, 1), (1, 2), (3, 1))
+GROUPS = ((0, 1), (1, 3))
 SPLITS = ((0, 256), (256, 384))
 
 PIECES = 8
@@ -191,21 +191,15 @@
         if i + 1 < chunks:
             score(0, i + 1)
         soften(0, i)
+    pass_on(2)
     passed[1].wait_recv()
     passed[3].wait_recv()
+    passed[2].wait_recv()
     score(1, 0)
     for i in range(chunks):
-        if i == 4:
-            pass_on(2)
         if i + 1 < chunks:
             score(1, i + 1)
         soften(1, i)
-    passed[2].wait_recv()
-    score(2, 0)
-    for i in range(chunks):
-        if i + 1 < chunks:
-            score(2, i + 1)
-        soften(2, i)
         join(i)
 
     d, asb, arb, bsb, brb = (d0, d1), (as0, as1), (ar0, ar1), (bs0, bs1), (br0, br1)
@@ -348,7 +342,7 @@
         pltpu.VMEM((rows, WIDE), bf16),
         pltpu.VMEM((rows, lat), bf16),
         pltpu.VMEM((rows, 128), f32),
-        *[pltpu.VMEM((keys // 2, CHUNK), f32) for _ in range(2)],
+        *[pltpu.VMEM((3 * keys // 4, CHUNK), f32) for _ in range(2)],
         *[pltpu.VMEM((keys, rows), f32) for _ in range(2)],
         *[pltpu.VMEM((8, rows), f32) for _ in range(2)],
         pltpu.VMEM((keys, rows), bf16),

time: 38.9 us -> 38.2 us (0.982)
  Pallas kernels: 38.2 us -> 37.5 us
    pallas_call x1, Pallas kernels: 36.7 us -> 36 us  [per_device(): pl.pallas_call(functools.partial(kernel, n_ctx, heads), out_shape=(pltpu....]
where the time goes in v5:
time: 38.2 us; the launch traced here: 38.1 us
  Pallas kernels  37.5 us (98%)
  between operations  0.64 us (2%)
    pallas_call x1, Pallas kernels, per_device(): pl.pallas_call(functools.partial(kernel, n_ctx, heads), out_shape=(pltpu....  36 us
    pallas_call x1, Pallas kernels, per_device(): pl.pallas_call(move, out_shape=tuple((jax.ShapeDtypeStruct(r.shape, r.dty...  1.49 us

profile of v5, /device:TPU:1, one launch (start us, length us, event | category | flops | bytes accessed | tf_op | source)
XLA Modules:
  0.0 38.1 jit_solution(16922316414225817112)
XLA Ops:
  0.6 36.0 %shard_map.93 = (bf16[2048,512]{1,0:T(8,128)(2,1)S(1)}, bf16[128,1024]{1,0:T(8,128)(2,1)S(1)}, bf16[32,512]{1,0:T(8,128)(2,1)S(1)}, bf16[32,64]{1,0:T(8,128)(2,1)S(1)}) custom-call(s32[128]{0:T(128)} %pos_hbm.1, bf16[128,512]{1,0:T(8,128)(2,1)} %kv_hbm.1, bf16[64,128]{1,0:T(8,128)(2,1)} %bitcast.7, bf16[128,1024]{1,0:T(8,128)(2,1)} %qr_hbm.1, ...), custom_call_target="tpu_custom_call" | custom-call | flops 6174015488 | bytes 7340032 | tf_op jit(solution)/shard_map/pallas_call | solution.py:362
  36.6 1.5 %shard_map.94 = (bf16[2048,512]{1,0:T(8,128)(2,1)}, bf16[128,1024]{1,0:T(8,128)(2,1)}, bf16[32,512]{1,0:T(8,128)(2,1)}, bf16[32,64]{1,0:T(8,128)(2,1)}) custom-call(bf16[2048,512]{1,0:T(8,128)(2,1)S(1)} %get-tuple-element.12.refs_0_, bf16[128,1024]{1,0:T(8,128)(2,1)S(1)} %get-tuple-element.13.refs_1_, bf16[32,512]{1,0:T(8,128)(2,1)S(1)} %get-tuple-element.14.refs_2_, ...), custom_call_target="tpu_custom_call" | custom-call | tf_op jit(solution)/shard_map/pallas_call | solution.py:384

commit v6 on v5

--- a/solution.py
+++ b/solution.py
@@ -188,10 +188,10 @@
         if i == 5:
             pass_on(1)
             pass_on(3)
+            pass_on(2)
         if i + 1 < chunks:
             score(0, i + 1)
         soften(0, i)
-    pass_on(2)
     passed[1].wait_recv()
     passed[3].wait_recv()
     passed[2].wait_recv()

time: 38.2 us -> 37.6 us (0.984)
  Pallas kernels: 37.5 us -> 36.9 us
    pallas_call x1, Pallas kernels: 36 us -> 35.4 us  [per_device(): pl.pallas_call(functools.partial(kernel, n_ctx, heads), out_shape=(pltpu....]
where the time goes in v6:
time: 37.6 us; the launch traced here: 37.5 us
  Pallas kernels  36.9 us (98%)
  between operations  0.64 us (2%)
    pallas_call x1, Pallas kernels, per_device(): pl.pallas_call(functools.partial(kernel, n_ctx, heads), out_shape=(pltpu....  35.4 us
    pallas_call x1, Pallas kernels, per_device(): pl.pallas_call(move, out_shape=tuple((jax.ShapeDtypeStruct(r.shape, r.dty...  1.49 us

profile of v6, /device:TPU:1, one launch (start us, length us, event | category | flops | bytes accessed | tf_op | source)
XLA Modules:
  0.0 37.5 jit_solution(15926091966390743563)
XLA Ops:
  0.6 35.4 %shard_map.93 = (bf16[2048,512]{1,0:T(8,128)(2,1)S(1)}, bf16[128,1024]{1,0:T(8,128)(2,1)S(1)}, bf16[32,512]{1,0:T(8,128)(2,1)S(1)}, bf16[32,64]{1,0:T(8,128)(2,1)S(1)}) custom-call(s32[128]{0:T(128)} %pos_hbm.1, bf16[128,512]{1,0:T(8,128)(2,1)} %kv_hbm.1, bf16[64,128]{1,0:T(8,128)(2,1)} %bitcast.7, bf16[128,1024]{1,0:T(8,128)(2,1)} %qr_hbm.1, ...), custom_call_target="tpu_custom_call" | custom-call | flops 6174015488 | bytes 7340032 | tf_op jit(solution)/shard_map/pallas_call | solution.py:362
  36.0 1.5 %shard_map.94 = (bf16[2048,512]{1,0:T(8,128)(2,1)}, bf16[128,1024]{1,0:T(8,128)(2,1)}, bf16[32,512]{1,0:T(8,128)(2,1)}, bf16[32,64]{1,0:T(8,128)(2,1)}) custom-call(bf16[2048,512]{1,0:T(8,128)(2,1)S(1)} %get-tuple-element.12.refs_0_, bf16[128,1024]{1,0:T(8,128)(2,1)S(1)} %get-tuple-element.13.refs_1_, bf16[32,512]{1,0:T(8,128)(2,1)S(1)} %get-tuple-element.14.refs_2_, ...), custom_call_target="tpu_custom_call" | custom-call | tf_op jit(solution)/shard_map/pallas_call | solution.py:384

commit v7 on v6

--- a/solution.py
+++ b/solution.py
@@ -86,7 +86,7 @@
         )
 
     forward = {}
-    for k in (1, 3, 2):
+    for k in (2, 1, 3):
         forward[k] = remote(
             kvr.at[0, a], kvr.at[PLACE[k], a], f_send.at[k - 1], f_recv.at[k - 1], (ctx_at(k), h)
         )

time: 37.6 us -> 37.8 us (level)
  no operation moved by 1% of the time
where the time goes in v7:
time: 37.8 us; the launch traced here: 37.7 us
  Pallas kernels  37.1 us (98%)
  between operations  0.64 us (2%)
    pallas_call x1, Pallas kernels, per_device(): pl.pallas_call(functools.partial(kernel, n_ctx, heads), out_shape=(pltpu....  35.6 us
    pallas_call x1, Pallas kernels, per_device(): pl.pallas_call(move, out_shape=tuple((jax.ShapeDtypeStruct(r.shape, r.dty...  1.49 us

profile of v7, /device:TPU:1, one launch (start us, length us, event | category | flops | bytes accessed | tf_op | source)
XLA Modules:
  0.0 37.7 jit_solution(4315225454631872541)
XLA Ops:
  0.6 35.6 %shard_map.93 = (bf16[2048,512]{1,0:T(8,128)(2,1)S(1)}, bf16[128,1024]{1,0:T(8,128)(2,1)S(1)}, bf16[32,512]{1,0:T(8,128)(2,1)S(1)}, bf16[32,64]{1,0:T(8,128)(2,1)S(1)}) custom-call(s32[128]{0:T(128)} %pos_hbm.1, bf16[128,512]{1,0:T(8,128)(2,1)} %kv_hbm.1, bf16[64,128]{1,0:T(8,128)(2,1)} %bitcast.7, bf16[128,1024]{1,0:T(8,128)(2,1)} %qr_hbm.1, ...), custom_call_target="tpu_custom_call" | custom-call | flops 6174015488 | bytes 7340032 | tf_op jit(solution)/shard_map/pallas_call | solution.py:362
  36.2 1.5 %shard_map.94 = (bf16[2048,512]{1,0:T(8,128)(2,1)}, bf16[128,1024]{1,0:T(8,128)(2,1)}, bf16[32,512]{1,0:T(8,128)(2,1)}, bf16[32,64]{1,0:T(8,128)(2,1)}) custom-call(bf16[2048,512]{1,0:T(8,128)(2,1)S(1)} %get-tuple-element.12.refs_0_, bf16[128,1024]{1,0:T(8,128)(2,1)S(1)} %get-tuple-element.13.refs_1_, bf16[32,512]{1,0:T(8,128)(2,1)S(1)} %get-tuple-element.14.refs_2_, ...), custom_call_target="tpu_custom_call" | custom-call | tf_op jit(solution)/shard_map/pallas_call | solution.py:384
